TPU v7x, 128 devices: a whole 4x4x4 slice. The times are simulated.
128 devices in a mesh: comp: 2 (over z_hi), tile: 64 (over y, z_lo, x, core).
Axes of the slice: x: 4, y: 4, z: 4 (z_hi: 2, z_lo: 2; z = z_hi * 2 + z_lo), core: 2. Of those that a mesh axis runs over, the one named last changes fastest.
Arguments:
- fields: float32 [2, 14, 64, 32768], P('comp', None, None, 'tile'), may hold values from -5 to 5
- velocity: float32 [2, 2, 14, 64, 32768], P('comp', None, None, None, 'tile'), may hold values from -3 to 3
- mixing: float32 [2, 13, 64, 32768], P('comp', None, None, 'tile'), may hold values from 0.1 to 3
- surface_mask: int32 [2, 64, 32768], P('comp', None, 'tile'), may hold values 0 or 1
- intersection_ids: int32 [2, 16384, 2], P('comp', 'tile'), may hold values from 0 to 16383, as said below
- intersection_weights: bfloat16 [2, 16384, 2, 128, 128], P('comp', 'tile'), may hold values from -0.375 to 0.375
Outputs:
- advanced: float32 [2, 14, 64, 32768], P('comp', None, None, 'tile')
- coupled: float32 [2, 2, 64, 32768], P('comp', None, None, 'tile')
Inputs may be any that keep to these rules, and one draw needn't show every extreme that they name: `intersection_ids`: the 2 sources of a destination block on tile t are blocks of the tiles t - 1, t and t + 1 (the last and the first tile lie beside each other); a source may repeat.
All inputs are finite; a program needn't handle non-finite values. No bound on the sum of `surface_mask` on one device may be relied on, other than what follows from the above.
Results may differ from a plain program's by a relative error of at most 0.0029.
Values may be sent and summed in bfloat16 or wider, within the bound.
A program may use at most 128 MiB of HBM per device.

v0:
```python
import functools
import math

import jax
import jax.numpy as jnp
import numpy as np
from jax import lax
from jax.experimental import pallas as pl
from jax.experimental.pallas import tpu as pltpu
from jax.sharding import PartitionSpec as P

LEV = 14
TILES = 8
SUB = 8
COLS = 512
LANES = 128
GROUPS = 4
BLOCKS = 256
N_TILE = 64
MESH = pl.DeviceIdType.MESH
F32 = jnp.float32
BF16 = jnp.bfloat16


def gll_table():
    nodes = [-1.0, -1.0 / math.sqrt(5.0), 1.0 / math.sqrt(5.0), 1.0]
    weights = [math.prod(nodes[i] - nodes[j] for j in range(4) if j != i) for i in range(4)]
    table = np.zeros((4, 4))
    for i in range(4):
        for j in range(4):
            if i == j:
                table[i, j] = sum(1.0 / (nodes[i] - nodes[k]) for k in range(4) if k != i)
            else:
                table[i, j] = weights[i] / weights[j] / (nodes[i] - nodes[j])
    return table


def along_matrix():
    full = np.kron(np.eye(LANES // 4), gll_table().T).astype(np.float32)
    return full


def across_table():
    table = gll_table()
    coefs = np.zeros((4, SUB, LANES), np.float32)
    for row in range(SUB):
        for m in range(4):
            coefs[m, row, :] = table[row % 4, m]
    return coefs


def kernel(
    ids_in, coef_in, deriv_in, fields, velocity, mixing, mask_in, weights,
    u, cpl,
    vel, kap, elim, msk, wbuf, surf, src, winb, win, st, work, inv,
    ids, pos_v, pos, coef, deriv, dmat, pack, dense, top, halo, sides_at, mirror,
    delta, delta_out, delta_in, delta_side,
    lsem, wsem, e0s, e0r, xs, xr,
):
    comp = lax.axis_index("comp")
    tile = lax.axis_index("tile")
    other = 1 - comp
    east = lax.rem(tile + 1, N_TILE)
    west = lax.rem(tile + N_TILE - 1, N_TILE)
    fold = N_TILE - 1 - tile
    fold_lo = lax.rem(fold + N_TILE - 1, N_TILE)
    fold_hi = lax.rem(fold + 1, N_TILE)
    is_atmos = comp == 0
    is_ocean = comp == 1
    level_s = jnp.where(is_atmos, LEV - 1, 0)
    spans = [slice(j * LANES, (j + 1) * LANES) for j in range(GROUPS)]

    def local(src_ref, dst_ref, sem):
        return pltpu.make_async_copy(src_ref, dst_ref, sem)

    def remote(src_ref, dst_ref, send, recv, target):
        return pltpu.make_async_remote_copy(
            src_ref=src_ref, dst_ref=dst_ref, send_sem=send, recv_sem=recv,
            device_id=target, device_id_type=MESH,
        )

    loads = [
        local(fields.at[level_s], surf.at[0], lsem.at[0]),
        local(velocity.at[0, level_s], surf.at[1], lsem.at[1]),
        local(fields, u, lsem.at[2]),
        local(mask_in, msk, lsem.at[3]),
        local(mixing, kap, lsem.at[4]),
        local(velocity, vel, lsem.at[5]),
        local(ids_in, ids, lsem.at[6]),
        local(coef_in, coef, lsem.at[7]),
        local(deriv_in, deriv, lsem.at[8]),
    ]
    order = (0, 3, 1, 2)
    wloads = [local(weights.at[:, :, j], wbuf.at[j], wsem.at[j]) for j in range(GROUPS)]
    for load in loads:
        load.start()

    for j in order:
        wloads[j].start()

    barrier = pltpu.get_barrier_semaphore()
    for target in (
        (other, tile), (comp, east), (comp, west), (comp, fold),
    ):
        pl.semaphore_signal(barrier, inc=1, device_id=target, device_id_type=MESH)

    @pl.when(fold_lo != tile)
    def _():
        pl.semaphore_signal(barrier, inc=1, device_id=(comp, fold_lo), device_id_type=MESH)

    @pl.when(fold_hi != tile)
    def _():
        pl.semaphore_signal(barrier, inc=1, device_id=(comp, fold_hi), device_id_type=MESH)

    loads[0].wait()
    loads[1].wait()
    for f in range(2):
        for j in range(GROUPS):
            src[f, j] = surf[f, :, :, spans[j]].reshape(64, LANES).astype(BF16)

    selfs = jnp.where(fold_lo == tile, 1, 0) + jnp.where(fold_hi == tile, 1, 0)
    pl.semaphore_wait(barrier, 6 - selfs)

    center = remote(src, winb.at[1], e0s.at[1], e0r.at[1], (other, tile))
    center.start()
    forwards = [
        remote(winb.at[1], winb.at[0], e0s.at[0], e0r.at[0], (comp, east)),
        remote(winb.at[1], winb.at[2], e0s.at[2], e0r.at[2], (comp, west)),
    ]

    lane = lax.broadcasted_iota(jnp.int32, (SUB, LANES), 1)
    row = lax.broadcasted_iota(jnp.int32, (SUB, LANES), 0)
    lane_w = lax.broadcasted_iota(jnp.int32, (SUB, COLS), 1)
    row_w = lax.broadcasted_iota(jnp.int32, (SUB, COLS), 0)
    flip = (LANES - 1) - lane
    low_half = lane < 64
    pair_lane = jnp.where(
        (lane & 3) == 3, (lane + 1) & (LANES - 1),
        jnp.where((lane & 3) == 0, (lane + LANES - 1) & (LANES - 1), lane),
    )
    pair_row = jnp.where(
        (row & 3) == 3, (row + 1) & 7, jnp.where((row & 3) == 0, (row + 7) & 7, row)
    )
    ends = jnp.where(low_half, 0, LANES - 1)
    element = row & 4

    def lanes_of(x, index):
        return jnp.take_along_axis(x, index, axis=1)

    def rows_of(x, index):
        return jnp.take_along_axis(x, index, axis=0)

    def row_pair_sum(x, following, previous):
        mixed = jnp.where(row == 0, following, jnp.where(row == SUB - 1, previous, x))
        return x + rows_of(mixed, pair_row)

    def column_pair_sum(ys, sides, groups=range(GROUPS)):
        result = {}
        for j in groups:
            after = ys[j + 1] if j < GROUPS - 1 else sides
            before = ys[j - 1] if j > 0 else sides
            mixed = jnp.where(lane == 0, after, jnp.where(lane == LANES - 1, before, ys[j]))
            result[j] = ys[j] + lanes_of(mixed, pair_lane)
        return result

    def factors(i, carry):
        above = None
        ratio = None
        for l in range(LEV):
            diagonal = 1.0
            if l < LEV - 1:
                below = kap[l, i]
                diagonal = below + 1.0
            if l > 0:
                diagonal = diagonal + above * (1.0 - ratio)
            inverse = 1.0 / diagonal
            inv[l, i] = inverse
            if l > 0:
                elim[l - 1, i] = above * inverse
            if l < LEV - 1:
                ratio = below * inverse
                above = below
                kap[l, i] = ratio
        return carry

    def tendency(units, heated):
        xs = [u[:, i, :, spans[j]] for i, j in units]
        flat = jnp.concatenate([x.reshape(LEV * SUB, LANES) for x in xs], axis=0)
        high = flat.astype(BF16)
        low = (flat - high.astype(F32)).astype(BF16)
        product = jnp.dot(
            jnp.concatenate([high, low], axis=1), dmat[...], preferred_element_type=F32
        )
        for n, (i, j) in enumerate(units):
            span = spans[j]
            part = product[n * LEV * SUB:(n + 1) * LEV * SUB]
            along = (part[:, :LANES] + part[:, LANES:]).reshape(LEV, SUB, LANES)
            for l in range(LEV):
                xl = xs[n][l]
                across = rows_of(xl, element) * coef[0]
                for m in range(1, 4):
                    across += rows_of(xl, element + m) * coef[m]
                value = xl - 0.08 * (
                    vel[0, l, i, :, span] * along[l] + vel[1, l, i, :, span] * across
                )
                if heated and l == LEV - 1:
                    value = value + heat_rate(i, span) * (cpl[0, i, :, span] - xl)
                st[l, i + 1, :, span] = value

    def rate_of(i, span, wind):
        wet = msk[i, :, span].astype(F32)
        return 0.5 * (1.0 + jnp.abs(surf[1, i, :, span] - wind)) * wet

    def heat_rate(i, span):
        return rate_of(i, span, cpl[1, i, :, span])

    def delta_at(i, span):
        return heat_rate(i, span) * (cpl[0, i, :, span] - surf[0, i, :, span])

    def turned(x, amount):
        amount = amount % LANES
        return x if amount == 0 else pltpu.roll(x, amount, 1)

    def side_pack(left, right):
        return lanes_of(jnp.where(lane == 0, left, right), ends)

    def pack_edges(values, shift, slot, with_mask):
        def body(i, carry):
            packed = jnp.zeros((SUB, LANES), F32)
            for l in range(LEV + with_mask):
                if l < LEV:
                    left = values[l, i + shift, :, spans[0]]
                    right = values[l, i + shift, :, spans[-1]]
                else:
                    left = msk[i, :, spans[0]].astype(F32)
                    right = msk[i, :, spans[-1]].astype(F32)
                packed = jnp.where((lane & 63) == l, side_pack(left, right), packed)
            pack[i] = packed
            return carry

        lax.fori_loop(0, TILES, body, 0, unroll=8)
        dense_w = jnp.zeros((SUB, LANES), F32)
        dense_e = jnp.zeros((SUB, LANES), F32)
        for i in range(TILES):
            here = lax.shift_right_logical(lane, 4) == i
            dense_w = jnp.where(here, turned(pack[i], 16 * i), dense_w)
            dense_e = jnp.where(here, turned(pack[i], 16 * i - 64), dense_e)
        dense[slot, 0] = dense_w
        dense[slot, 1] = dense_e
        for half in range(2):
            for j in range(GROUPS):
                rows = []
                for s in range(8):
                    l = half * 8 + s
                    if l < LEV:
                        rows.append(values[l, TILES - 1 + shift, 7:8, spans[j]])
                    elif l == LEV:
                        rows.append(msk[TILES - 1, 7:8, spans[j]].astype(F32))
                    else:
                        rows.append(jnp.zeros((1, LANES), F32))
                block = jnp.concatenate(rows, axis=0)
                top[slot, half * 8:half * 8 + 8, spans[GROUPS - 1 - j]] = lanes_of(block, flip)

    def exchange(base, to_west, to_east, to_fold, to_lo, to_hi, at):
        copies = [
            remote(to_fold, at[2], xs.at[base + 2], xr.at[base + 2], (comp, fold)),
            remote(to_west, at[0], xs.at[base], xr.at[base], (comp, west)),
            remote(to_east, at[1], xs.at[base + 1], xr.at[base + 1], (comp, east)),
        ]
        lo = remote(to_lo, at[3], xs.at[base + 3], xr.at[base + 3], (comp, fold_lo))
        hi = remote(to_hi, at[4], xs.at[base + 4], xr.at[base + 4], (comp, fold_hi))

        def start():
            for copy in copies:
                copy.start()

            @pl.when(fold_lo != tile)
            def _():
                lo.start()

            @pl.when(fold_hi != tile)
            def _():
                hi.start()

            @pl.when(fold_lo == tile)
            def _():
                at[3][...] = to_lo[...]

            @pl.when(fold_hi == tile)
            def _():
                at[4][...] = to_hi[...]

        def wait():
            for copy in copies:
                copy.wait_recv()

            @pl.when(fold_lo != tile)
            def _():
                lo.wait_recv()

            @pl.when(fold_hi != tile)
            def _():
                hi.wait_recv()

        def drain():
            for copy in copies:
                copy.wait_send()

            @pl.when(fold_lo != tile)
            def _():
                lo.wait_send()

            @pl.when(fold_hi != tile)
            def _():
                hi.wait_send()

        return start, wait, drain

    def halo_exchange(slot):
        return exchange(
            slot * 5, dense.at[slot, 0], dense.at[slot, 1], top.at[slot],
            dense.at[slot, 1], dense.at[slot, 0],
            [halo.at[slot, 0], halo.at[slot, 1], mirror.at[slot], halo.at[slot, 2], halo.at[slot, 3]],
        )

    def delta_exchange():
        return exchange(
            10, delta_out.at[0], delta_out.at[0], delta_out.at[1], delta_out.at[2], delta_out.at[2],
            [delta_in.at[n] for n in range(5)],
        )

    def fill_south():
        for l in range(LEV):
            st[l, 0, 7:8, :] = st[l, 1, 0:1, :]

    def fill_north(slot):
        for l in range(LEV):
            st[l, TILES + 1, 0:1, :] = mirror[slot, l:l + 1, :]

    def spread_sides(slot, summed):
        both = []
        for n in range(2):
            h = halo[slot, n]
            if summed:
                corner = pltpu.roll(halo[slot, 2 + n], 1, 0)
                following = jnp.where(lane >= LANES - 16, corner, turned(h, -16))
                previous = jnp.where(
                    lane < 16, jnp.broadcast_to(h[0:1], (SUB, LANES)), turned(h, 16)
                )
                h = row_pair_sum(h, following, previous)
            both.append(h)
        for i in range(TILES):
            sides_at[slot, i] = jnp.where(
                low_half, turned(both[0], -16 * i), turned(both[1], 64 - 16 * i)
            )

    def side_pick(halos, l):
        return lanes_of(halos, jnp.where(low_half, l, 64 + l))

    def row_sums(l, i):
        return [
            row_pair_sum(st[l, i + 1, :, span], st[l, i + 2, :, span], st[l, i, :, span])
            for span in spans
        ]

    def eliminate(i, l, j, value, carried):
        value = value * inv[l, i, :, spans[j]]
        if l > 0:
            value = value + elim[l - 1, i, :, spans[j]] * carried
        return value

    def back_substitute(i, j, partial):
        span = spans[j]
        result = partial[LEV - 1]
        u[LEV - 1, i, :, span] = result
        for l in range(LEV - 2, -1, -1):
            result = partial[l] + kap[l, i, :, span] * result
            u[l, i, :, span] = result

    def forward_first(i, carry):
        halos = sides_at[0, i]
        carried = [None] * GROUPS
        for l in range(LEV):
            sums = column_pair_sum(row_sums(l, i), side_pick(halos, l))
            for j in range(GROUPS):
                carried[j] = 0.25 * sums[j]
                if l < LEV - 1:
                    carried[j] = eliminate(i, l, j, carried[j], previous[j] if l else None)
                work[l, i, :, spans[j]] = carried[j]
            previous = list(carried)
        return carry

    def finish_first(i, groups):
        ys = [
            row_pair_sum(delta[i + 1, :, span], delta[i + 2, :, span], delta[i, :, span])
            for span in spans
        ]
        sums = column_pair_sum(ys, delta_side[i], groups)
        for j in groups:
            span = spans[j]
            partial = [work[l, i, :, span] for l in range(LEV - 1)]
            value = work[LEV - 1, i, :, span] + 0.25 * sums[j]
            partial.append(eliminate(i, LEV - 1, j, value, partial[-1]))
            back_substitute(i, j, partial)

    def finish_second(i, groups, ys_at, halos):
        carried = {j: None for j in groups}
        partial = {j: [] for j in groups}
        for l in range(LEV):
            sides = halos if halos is None else side_pick(halos, l)
            sums = column_pair_sum(ys_at(l), sides, groups)
            for j in groups:
                carried[j] = eliminate(i, l, j, 0.25 * sums[j], carried[j])
                partial[j].append(carried[j])
        for j in groups:
            back_substitute(i, j, partial[j])

    def second_middle(i, carry):
        def ys_at(l):
            ys = row_sums(l, i)
            for j in range(GROUPS):
                work[l, i, :, spans[j]] = ys[j]
            return ys

        finish_second(i, (1, 2), ys_at, None)
        return carry

    def second_sides(i, carry):
        def ys_at(l):
            return [work[l, i, :, span] for span in spans]

        finish_second(i, (0, 3), ys_at, sides_at[1, i])
        return carry

    def beside(x, left, right):
        from_east = jnp.where(lane_w == COLS - 1, right, pltpu.roll(x, COLS - 1, 1))
        from_west = jnp.where(lane_w == 0, left, pltpu.roll(x, 1, 1))
        return from_east, from_west

    def beyond(x, nxt, prev):
        upper = jnp.where(row_w == 7, jnp.broadcast_to(nxt, (SUB, COLS)), pltpu.roll(x, 7, 0))
        lower = jnp.where(row_w == 0, jnp.broadcast_to(prev, (SUB, COLS)), pltpu.roll(x, 1, 0))
        return upper, lower

    def ocean_sides(slot, i, l):
        right = jnp.broadcast_to(sides_at[slot, i, :, l:l + 1], (SUB, COLS))
        left = jnp.broadcast_to(sides_at[slot, i, :, 64 + l:65 + l], (SUB, COLS))
        return left, right

    def ocean_masks(i):
        wet = msk[i].astype(F32)
        m_e, m_w = beside(wet, *ocean_sides(0, i, LEV))
        nxt = jnp.where(
            i == TILES - 1, mirror[0, LEV:LEV + 1, :],
            msk[jnp.minimum(i + 1, TILES - 1), 0:1, :].astype(F32),
        )
        prev = jnp.where(i == 0, 0.0, msk[jnp.maximum(i - 1, 0), 7:8, :].astype(F32))
        m_n, m_s = beyond(wet, nxt, prev)
        return wet * m_e, wet * m_w, wet * m_n, wet * m_s

    def ocean_change(a, e, w, n, s, l, i, masks):
        d_e = masks[0] * (e - a)
        d_w = masks[1] * (w - a)
        d_n = masks[2] * (n - a)
        d_s = masks[3] * (s - a)
        return 0.15 * (d_e + d_w + d_n + d_s) - 0.25 * (
            vel[0, l, i] * (d_e - d_w) + vel[1, l, i] * (d_n - d_s)
        )

    def ocean_first(i, carry):
        masks = ocean_masks(i)
        for l in range(LEV):
            a = u[l, i]
            nxt = jnp.where(
                i == TILES - 1, mirror[0, l:l + 1, :], u[l, jnp.minimum(i + 1, TILES - 1), 0:1, :]
            )
            prev = jnp.where(i == 0, a[0:1], u[l, jnp.maximum(i - 1, 0), 7:8, :])
            e, w = beside(a, *ocean_sides(0, i, l))
            n, s = beyond(a, nxt, prev)
            change = ocean_change(a, e, w, n, s, l, i, masks)
            work[l, i] = change
            st[l, i + 1] = a + change
        return carry

    def ocean_second(i, carry):
        masks = ocean_masks(i)
        partial = [[] for _ in range(GROUPS)]
        carried = [None] * GROUPS
        for l in range(LEV):
            a = st[l, i + 1]
            e, w = beside(a, *ocean_sides(1, i, l))
            n, s = beyond(a, st[l, i + 2, 0:1, :], st[l, i, 7:8, :])
            change = ocean_change(a, e, w, n, s, l, i, masks)
            value = u[l, i] + 0.5 * (work[l, i] + change)
            if l == 0:
                value = value + delta[i + 1]
            for j in range(GROUPS):
                carried[j] = eliminate(i, l, j, value[:, spans[j]], carried[j])
                partial[j].append(carried[j])
        for j in range(GROUPS):
            back_substitute(i, j, partial[j])
        return carry

    for load in loads[2:9]:
        load.wait()
    high = deriv[...].astype(BF16)
    dmat[0:LANES, 0:LANES] = high
    dmat[0:LANES, LANES:2 * LANES] = (deriv[...] - high.astype(F32)).astype(BF16)
    dmat[LANES:2 * LANES, 0:LANES] = high
    dmat[LANES:2 * LANES, LANES:2 * LANES] = jnp.zeros((LANES, LANES), BF16)

    start_0, wait_0, drain_0 = halo_exchange(0)
    start_1, wait_1, drain_1 = halo_exchange(1)
    start_d, wait_d, drain_d = delta_exchange()

    @pl.when(is_ocean)
    def _():
        pack_edges(u, 0, 0, 1)
        start_0()

    def first_tendency(p, carry):
        tendency([(2 * p + r, j) for r in range(2) for j in range(GROUPS)], False)
        return carry

    @pl.when(is_atmos)
    def _():
        lax.fori_loop(0, TILES // 2, first_tendency, 0)
        pack_edges(st, 1, 0, 0)
        start_0()

    center.wait_recv()
    for copy in forwards:
        copy.start()

    lax.fori_loop(0, TILES, factors, 0, unroll=2)

    ident = ids[...]
    relative = (lax.shift_right_logical(ident, 8) - tile + 1 + N_TILE) & (N_TILE - 1)
    block = ident & (BLOCKS - 1)
    pos_v[...] = (
        jnp.minimum(relative, 2) * BLOCKS + (block & 3) * 64 + lax.shift_right_logical(block, 2)
    )
    pos_copy = local(pos_v, pos, lsem.at[9])
    pos_copy.start()

    pos_copy.wait()

    def widen(slot):
        for f in range(2):
            win[f, slot * BLOCKS:(slot + 1) * BLOCKS, :] = (
                winb[slot, f].reshape(BLOCKS, LANES).astype(F32)
            )

    widen(1)

    @pl.when(is_atmos)
    def _():
        wait_0()
        spread_sides(0, True)
        fill_south()
        fill_north(0)
        lax.fori_loop(0, TILES, forward_first, 0, unroll=4)

    @pl.when(is_ocean)
    def _():
        wait_0()
        spread_sides(0, False)
        lax.fori_loop(0, TILES, ocean_first, 0)
        pack_edges(st, 1, 1, 0)
        start_1()

    for copy in forwards:
        copy.wait_recv()
    widen(0)
    widen(2)

    def regrid_rows(j, b, rows_in):
        for s in rows_in:
            block = (b * 8 + s) * GROUPS + j
            sides = []
            for k in range(2):
                p = pos[k, block]
                rows = [win[0, pl.ds(p, 1), :], win[1, pl.ds(p, 1), :]]
                sides.append(jnp.concatenate(rows + rows[:1] * 6, axis=0))
            picked = jnp.concatenate(sides, axis=1).astype(BF16)
            tiles = jnp.concatenate([wbuf[j, b, s, 0], wbuf[j, b, s, 1]], axis=1)
            result = lax.dot_general(
                picked, tiles, (((1,), (1,)), ((), ())), preferred_element_type=F32
            )
            cpl[0, b, s:s + 1, spans[j]] = result[0:1]
            cpl[1, b, s:s + 1, spans[j]] = result[1:2]

    def regrid(j):
        def body(b, carry):
            regrid_rows(j, b, range(8))
            return carry

        lax.fori_loop(0, TILES, body, 0, unroll=8)

    for j in order:
        wloads[j].wait()

    def edge_delta(i, j, rows, pick):
        sums = [[], []]
        for s in range(SUB):
            block = (i * SUB + s) * GROUPS + j
            lines = [wbuf[j, i, s, k, rows, :].astype(F32)[pick:pick + 1] for k in range(2)]
            for f in range(2):
                sums[f].append(
                    lines[0] * win[f, pl.ds(pos[0, block], 1), :]
                    + lines[1] * win[f, pl.ds(pos[1, block], 1), :]
                )
        target, wind = [
            jnp.broadcast_to(
                jnp.sum(jnp.concatenate(part, axis=0), axis=1, keepdims=True), (SUB, LANES)
            )
            for part in sums
        ]
        return rate_of(i, spans[j], wind) * (target - surf[0, i, :, spans[j]])

    def edge_pack(i, packed):
        left = edge_delta(i, 0, slice(0, 16), 0)
        right = edge_delta(i, GROUPS - 1, slice(LANES - 16, LANES), 15)
        return jnp.where((lane & 63) == i, side_pack(left, right), packed)

    for j in range(GROUPS):
        regrid_rows(j, TILES - 1, (SUB - 1,))
    rows = [delta_at(TILES - 1, spans[j])[7:8] for j in range(GROUPS - 1, -1, -1)]
    delta_out[1] = lanes_of(jnp.concatenate(rows + rows, axis=0), flip)
    packed = lax.fori_loop(0, TILES, edge_pack, jnp.zeros((SUB, LANES), F32), unroll=4)
    delta_out[0] = packed
    delta_out[2, 0:1, :] = pltpu.roll(packed, 64, 1)[SUB - 1:SUB]
    start_d()
    for j in order:
        regrid(j)

    def all_delta(i, carry):
        for span in spans:
            delta[i + 1, :, span] = delta_at(i, span)
        return carry

    lax.fori_loop(0, TILES, all_delta, 0)

    wait_d()
    sides = jnp.where(low_half, delta_in[0], delta_in[1])
    for j in range(GROUPS):
        delta[TILES + 1, 0:1, spans[j]] = delta_in[2, j:j + 1, :]
    delta[0, 7:8, :] = delta[1, 0:1, :]

    @pl.when(is_atmos)
    def _():
        corner = jnp.where(low_half, delta_in[3], delta_in[4])
        following = jnp.where((lane & 63) == TILES - 1, corner, pltpu.roll(sides, LANES - 1, 1))
        previous = jnp.where(
            (lane & 63) == 0, jnp.broadcast_to(sides[0:1], (SUB, LANES)), pltpu.roll(sides, 1, 1)
        )
        summed = row_pair_sum(sides, following, previous)
        for i in range(TILES):
            delta_side[i] = side_pick(summed, i)

        last = TILES - 1

        def finish_sides(i, carry):
            finish_first(i, (0, 3))
            return carry

        def finish_inner(i, carry):
            finish_first(i, (1, 2))
            return carry

        def tend_sides(p, carry):
            tendency([(4 * p + r, j) for r in range(4) for j in (0, 3)], True)
            return carry

        def tend_inner(p, carry):
            tendency([(4 * p + r, j) for r in range(4) for j in (1, 2)], True)
            return carry

        lax.fori_loop(0, TILES, finish_sides, 0, unroll=4)
        finish_first(last, (1, 2))
        tendency([(last, 1), (last, 2)], True)
        lax.fori_loop(0, TILES // 4, tend_sides, 0)
        pack_edges(st, 1, 1, 0)
        start_1()
        lax.fori_loop(0, last, finish_inner, 0, unroll=7)
        lax.fori_loop(0, TILES // 4, tend_inner, 0)
        fill_south()
        lax.fori_loop(0, last, second_middle, 0, unroll=7)
        wait_1()
        spread_sides(1, True)
        fill_north(1)
        for l in range(LEV):
            ys = row_sums(l, last)
            for j in range(GROUPS):
                work[l, last, :, spans[j]] = ys[j]
        lax.fori_loop(0, TILES, second_sides, 0, unroll=4)
        finish_second(last, (1, 2), lambda l: [work[l, last, :, span] for span in spans], None)

    @pl.when(is_ocean)
    def _():
        wait_1()

        def add_forcing(i, carry):
            st[0, i + 1] = st[0, i + 1] + delta[i + 1]
            return carry

        lax.fori_loop(0, TILES, add_forcing, 0)
        mirror[1, 0:1, :] = mirror[1, 0:1, :] + delta[TILES + 1, 0:1, :]
        fill_south()
        fill_north(1)
        spread_sides(1, False)
        for i in range(TILES):
            sides_at[1, i] = sides_at[1, i] + jnp.where(
                (lane & 63) == 0, side_pick(sides, i), 0.0
            )
        lax.fori_loop(0, TILES, ocean_second, 0)

    center.wait_send()
    for copy in forwards:
        copy.wait_send()
    drain_0()
    drain_d()
    drain_1()


def on_device(fields, velocity, mixing, surface_mask, intersection_ids, intersection_weights):
    vmem = pl.BlockSpec(memory_space=pltpu.VMEM)
    hbm = pl.BlockSpec(memory_space=pltpu.HBM)
    scratch = [
        pltpu.VMEM((2, LEV, TILES, SUB, COLS), F32),
        pltpu.VMEM((LEV - 1, TILES, SUB, COLS), F32),
        pltpu.VMEM((LEV - 1, TILES, SUB, COLS), F32),
        pltpu.VMEM((TILES, SUB, COLS), jnp.int32),
        pltpu.VMEM((GROUPS, TILES, SUB, 2, LANES, LANES), BF16),
        pltpu.VMEM((2, TILES, SUB, COLS), F32),
        pltpu.VMEM((2, GROUPS, 64, LANES), BF16),
        pltpu.VMEM((3, 2, GROUPS, 64, LANES), BF16),
        pltpu.VMEM((2, 3 * BLOCKS, LANES), F32),
        pltpu.VMEM((LEV, TILES + 2, SUB, COLS), F32),
        pltpu.VMEM((LEV, TILES, SUB, COLS), F32),
        pltpu.VMEM((LEV, TILES, SUB, COLS), F32),
        pltpu.VMEM((2, BLOCKS), jnp.int32),
        pltpu.VMEM((2, BLOCKS), jnp.int32),
        pltpu.SMEM((2, BLOCKS), jnp.int32),
        pltpu.VMEM((4, SUB, LANES), F32),
        pltpu.VMEM((LANES, LANES), F32),
        pltpu.VMEM((2 * LANES, 2 * LANES), BF16),
        pltpu.VMEM((TILES, SUB, LANES), F32),
        pltpu.VMEM((2, 2, SUB, LANES), F32),
        pltpu.VMEM((2, 16, COLS), F32),
        pltpu.VMEM((2, 4, SUB, LANES), F32),
        pltpu.VMEM((2, TILES, SUB, LANES), F32),
        pltpu.VMEM((2, 16, COLS), F32),
        pltpu.VMEM((TILES + 2, SUB, COLS), F32),
        pltpu.VMEM((3, SUB, LANES), F32),
        pltpu.VMEM((5, SUB, LANES), F32),
        pltpu.VMEM((TILES, SUB, LANES), F32),
        pltpu.SemaphoreType.DMA((10,)),
        pltpu.SemaphoreType.DMA((GROUPS,)),
        pltpu.SemaphoreType.DMA((3,)),
        pltpu.SemaphoreType.DMA((3,)),
        pltpu.SemaphoreType.DMA((15,)),
        pltpu.SemaphoreType.DMA((15,)),
    ]
    advanced, coupled = pl.pallas_call(
        kernel,
        out_shape=(
            pltpu.VMEM((LEV, TILES, SUB, COLS), F32),
            pltpu.VMEM((2, TILES, SUB, COLS), F32),
        ),
        in_specs=[hbm] * 8,
        out_specs=(vmem, vmem),
        scratch_shapes=scratch,
        compiler_params=pltpu.CompilerParams(
            collective_id=0, has_side_effects=True, vmem_limit_bytes=52 << 20
        ),
    )(
        jnp.transpose(intersection_ids[0], (1, 0)),
        jnp.asarray(across_table()),
        jnp.asarray(along_matrix()),
        fields.reshape(LEV, TILES, SUB, COLS),
        velocity.reshape(2, LEV, TILES, SUB, COLS),
        mixing.reshape(LEV - 1, TILES, SUB, COLS),
        surface_mask.reshape(TILES, SUB, COLS),
        intersection_weights.reshape(TILES, SUB, GROUPS, 2, LANES, LANES),
    )
    return (
        advanced.reshape(1, LEV, TILES * SUB, COLS),
        coupled.reshape(1, 2, TILES * SUB, COLS),
    )


def solution(mesh):
    placed = (
        P("comp", None, None, "tile"),
        P("comp", None, None, None, "tile"),
        P("comp", None, None, "tile"),
        P("comp", None, "tile"),
        P("comp", "tile", None),
        P("comp", "tile", None, None, None),
    )
    return jax.shard_map(
        on_device,
        mesh=mesh,
        in_specs=placed,
        out_specs=(P("comp", None, None, "tile"), P("comp", None, None, "tile")),
        check_vma=False,
    )
```

profile of v0, /device:TPU:1, one launch (start us, length us, event | category | flops | bytes accessed | tf_op | source)
XLA Modules:
  0.0 39.1 jit_solution(6261663408895185200)
XLA Ops:
  0.6 36.5 %shard_map.95 = (f32[14,8,8,512]{3,2,1,0:T(8,128)S(1)}, f32[2,8,8,512]{3,2,1,0:T(8,128)S(1)}) custom-call(s32[2,256]{1,0:T(2,128)} %bitcast.17, f32[4,8,128]{2,1,0:T(8,128)} %constant.4.clone.coef_in, f32[128,128]{1,0:T(8,128)} %constant.5.clone.deriv_in, f32[14,8,8,512]{3,2,1,0:T(8,128)} %bitcast.14, f32[2,14,8,8,512]{4,3,2,1,0:T(8,128)} %bitcast.13, ...), custom_call_target="tpu_custom_call" | custom-call | tf_op jit(solution)/shard_map/pallas_call | solution.py:765
  37.2 1.2 %copy.12 = f32[1,14,64,512]{3,2,1,0:T(8,128)} copy(f32[1,14,64,512]{3,2,1,0:T(8,128)S(1)} %bitcast.10) | data formatting | bytes 3670016
  38.4 0.7 %copy.13 = f32[1,2,64,512]{3,2,1,0:T(8,128)} copy(f32[1,2,64,512]{3,2,1,0:T(8,128)S(1)} %bitcast.11) | data formatting | bytes 524288
where the time goes:
time: 39.2 us; the launch traced here: 39.1 us
  Pallas kernels  36.5 us (93%)
  local copies, waits for them, and re-layouts  1.93 us (5%)
  between operations  0.64 us (2%)
    pallas_call x1, Pallas kernels, on_device(): pl.pallas_call(kernel, out_shape=(pltpu.VMEM((LEV, TILES, SUB, COLS), F32...  36.5 us
    unnamed x2, local copies, waits for them, and re-layouts  1.93 us

commit v1 on v0

--- a/solution.py
+++ b/solution.py
@@ -92,8 +92,8 @@
     ]
     order = (0, 3, 1, 2)
     wloads = [local(weights.at[:, :, j], wbuf.at[j], wsem.at[j]) for j in range(GROUPS)]
-    for load in loads:
-        load.start()
+    for n in (0, 1, 2, 5, 8, 7, 3, 4, 6):
+        loads[n].start()
 
     for j in order:
         wloads[j].start()
@@ -501,8 +501,8 @@
             back_substitute(i, j, partial[j])
         return carry
 
-    for load in loads[2:9]:
-        load.wait()
+    for n in (2, 3, 5, 7, 8):
+        loads[n].wait()
     high = deriv[...].astype(BF16)
     dmat[0:LANES, 0:LANES] = high
     dmat[0:LANES, LANES:2 * LANES] = (deriv[...] - high.astype(F32)).astype(BF16)
@@ -519,12 +519,12 @@
         start_0()
 
     def first_tendency(p, carry):
-        tendency([(2 * p + r, j) for r in range(2) for j in range(GROUPS)], False)
+        tendency([(4 * p + r, j) for r in range(4) for j in range(GROUPS)], False)
         return carry
 
     @pl.when(is_atmos)
     def _():
-        lax.fori_loop(0, TILES // 2, first_tendency, 0)
+        lax.fori_loop(0, TILES // 4, first_tendency, 0)
         pack_edges(st, 1, 0, 0)
         start_0()
 
@@ -532,6 +532,8 @@
     for copy in forwards:
         copy.start()
 
+    loads[4].wait()
+    loads[6].wait()
     lax.fori_loop(0, TILES, factors, 0, unroll=2)
 
     ident = ids[...]

time: 39.2 us -> 39.9 us (1.018)
  Pallas kernels: 36.5 us -> 37.3 us
    pallas_call x1, Pallas kernels: 36.5 us -> 37.3 us  [on_device(): pl.pallas_call(kernel, out_shape=(pltpu.VMEM((LEV, TILES, SUB, COLS), F32...]
where the time goes in v1:
time: 39.9 us; the launch traced here: 39.8 us
  Pallas kernels  37.3 us (93%)
  local copies, waits for them, and re-layouts  1.93 us (5%)
  between operations  0.64 us (2%)
    pallas_call x1, Pallas kernels, on_device(): pl.pallas_call(kernel, out_shape=(pltpu.VMEM((LEV, TILES, SUB, COLS), F32...  37.3 us
    unnamed x2, local copies, waits for them, and re-layouts  1.93 us

profile of v1, /device:TPU:1, one launch (start us, length us, event | category | flops | bytes accessed | tf_op | source)
XLA Modules:
  0.0 39.8 jit_solution(926988699768963822)
XLA Ops:
  0.6 37.3 %shard_map.95 = (f32[14,8,8,512]{3,2,1,0:T(8,128)S(1)}, f32[2,8,8,512]{3,2,1,0:T(8,128)S(1)}) custom-call(s32[2,256]{1,0:T(2,128)} %bitcast.17, f32[4,8,128]{2,1,0:T(8,128)} %constant.4.clone.coef_in, f32[128,128]{1,0:T(8,128)} %constant.5.clone.deriv_in, f32[14,8,8,512]{3,2,1,0:T(8,128)} %bitcast.14, f32[2,14,8,8,512]{4,3,2,1,0:T(8,128)} %bitcast.13, ...), custom_call_target="tpu_custom_call" | custom-call | tf_op jit(solution)/shard_map/pallas_call | solution.py:767
  37.9 1.2 %copy.12 = f32[1,14,64,512]{3,2,1,0:T(8,128)} copy(f32[1,14,64,512]{3,2,1,0:T(8,128)S(1)} %bitcast.10) | data formatting | bytes 3670016
  39.1 0.7 %copy.13 = f32[1,2,64,512]{3,2,1,0:T(8,128)} copy(f32[1,2,64,512]{3,2,1,0:T(8,128)S(1)} %bitcast.11) | data formatting | bytes 524288
